TPU v7x, 256 devices: a whole 4x4x8 slice. The times are simulated.
256 devices in a mesh: dp: 32 (over y, z_lo, core), seq: 8 (over z_hi, x).
Axes of the slice: x: 4, y: 4, z: 8 (z_hi: 2, z_lo: 4; z = z_hi * 4 + z_lo), core: 2. Of those that a mesh axis runs over, the one named last changes fastest.
Arguments:
- x_img: bfloat16 [32, 1024, 3072], P('dp', 'seq'), may hold values from -6 to 6
- txt_qkv: bfloat16 [32, 128, 6144], P('dp', None, 'seq'), may hold values from -6 to 6
- w_qkv: bfloat16 [3072, 6144], P('dp', 'seq'), may hold values from -0.109375 to 0.109375
- q_gain: float32 [128], replicated, may hold values from 0.5 to 1.5
- k_gain: float32 [128], replicated, may hold values from 0.5 to 1.5
- d_out: bfloat16 [32, 1152, 2048], P('dp', None, 'seq'), may hold values from -6 to 6
Outputs:
- grad_w: float32 [3072, 6144], P('dp', 'seq')
- grad_txt: bfloat16 [32, 128, 6144], P('dp', None, 'seq')
All inputs are finite; a program needn't handle non-finite values.
Results may differ from a plain program's by a relative error of at most 0.03.
Values may be sent and summed in bfloat16 or wider, within the bound.
A program may use at most 64 MiB of HBM per device.

v0:
```python
import jax
import jax.numpy as jnp
from jax import lax
from jax.sharding import PartitionSpec as P


def head_grads(query_rows, key_rows, value_rows, grad_rows, q_gain, k_gain):
    scaling = query_rows.shape[-1] ** (-0.5)
    query_f = query_rows.astype(jnp.float32)
    key_f = key_rows.astype(jnp.float32)
    query_inv = lax.rsqrt(jnp.mean(query_f * query_f, -1, keepdims=True) + 1e-06)
    key_inv = lax.rsqrt(jnp.mean(key_f * key_f, -1, keepdims=True) + 1e-06)
    query_unit = query_f * query_inv
    key_unit = key_f * key_inv
    query_norm = (query_unit * q_gain).astype(jnp.bfloat16)
    key_norm = (key_unit * k_gain).astype(jnp.bfloat16)
    scores = jnp.dot(query_norm, key_norm.T, preferred_element_type=jnp.float32) * scaling
    powers = jnp.exp(scores)
    softmax = powers / jnp.sum(powers, -1, keepdims=True)
    softmax_low = softmax.astype(jnp.bfloat16)
    value_grad = jnp.dot(softmax_low.T, grad_rows, preferred_element_type=jnp.float32)
    prob_grad = jnp.dot(grad_rows, value_rows.T, preferred_element_type=jnp.float32)
    centre = jnp.sum(softmax * prob_grad, -1, keepdims=True)
    score_grad = (softmax * (prob_grad - centre) * scaling).astype(jnp.bfloat16)
    qnorm_grad = jnp.dot(score_grad, key_norm, preferred_element_type=jnp.float32) * q_gain
    knorm_grad = jnp.dot(score_grad.T, query_norm, preferred_element_type=jnp.float32) * k_gain
    query_grad = query_inv * (
        qnorm_grad - query_unit * jnp.mean(qnorm_grad * query_unit, -1, keepdims=True)
    )
    key_grad = key_inv * (
        knorm_grad - key_unit * jnp.mean(knorm_grad * key_unit, -1, keepdims=True)
    )
    return jnp.stack([query_grad, key_grad, value_grad], 1).astype(jnp.bfloat16)


def attention_grads(joined, grad_out, q_gain, k_gain, head_count):
    length_all = joined.shape[0]
    stacked = joined.reshape(length_all, head_count, 3, -1).transpose(1, 0, 2, 3)
    grad_heads = grad_out.reshape(length_all, head_count, -1).transpose(1, 0, 2)

    def single_head(items):
        return head_grads(items[0][:, 0], items[0][:, 1], items[0][:, 2], items[1], q_gain, k_gain)

    result = lax.map(single_head, (stacked, grad_heads))
    return result.transpose(1, 0, 2, 3).reshape(length_all, -1)


def per_device(x_img, txt_qkv, w_qkv, q_gain, k_gain, d_out):
    image_rows = x_img[0]
    head_size = q_gain.shape[0]
    head_count = d_out.shape[2] // head_size
    gathered = lax.all_gather(image_rows, "seq", axis=0, tiled=True)
    slab_part = gathered
    projected = jnp.dot(
        slab_part,
        lax.all_gather(w_qkv, "dp", axis=0, tiled=True),
        preferred_element_type=jnp.float32,
    )
    joined = jnp.concatenate([txt_qkv[0], projected.astype(jnp.bfloat16)], 0)
    text_length = txt_qkv.shape[1]
    qkv_grad = attention_grads(joined, d_out[0], q_gain, k_gain, head_count)
    image_grad = qkv_grad[text_length:]
    slab_part = gathered
    grad_w = lax.psum_scatter(
        lax.dot_general(
            slab_part, image_grad, (((0,), (0,)), ((), ())), preferred_element_type=jnp.float32
        ).astype(jnp.bfloat16),
        "dp",
        scatter_dimension=0,
        tiled=True,
    ).astype(jnp.float32)
    text_grad = qkv_grad[:text_length]
    return (grad_w, text_grad[None])


def solution(mesh):
    in_specs = (
        P("dp", "seq", None),
        P("dp", None, "seq"),
        P("dp", "seq"),
        P(),
        P(),
        P("dp", None, "seq"),
    )
    out_specs = (P("dp", "seq"), P("dp", None, "seq"))
    return jax.shard_map(
        per_device, mesh=mesh, in_specs=in_specs, out_specs=out_specs, check_vma=False
    )
```

profile of v0, /device:TPU:1, one launch (start us, length us, event | category | flops | bytes accessed | tf_op | source)
XLA Modules:
  0.0 410.1 jit_solution(637955431180120441)
XLA Ops:
  7.2 0.0 all-gather.4.cloned.1.call-start
  7.2 0.7 all-gather.4.cloned.1.call-update
  7.9 0.0 all-gather.6.cloned.1.call-start
  7.9 0.7 all-gather.6.cloned.1.call-update
  8.6 0.0 reduce-scatter.4.cloned.1.call-start
  8.7 1.7 copy.19
  10.4 2.1 copy.20
  12.6 0.0 copy-start.1
  12.6 0.0 copy-start.2
  12.6 65.5 %all-gather.4.cloned.1.call-done = bf16[3072,768]{1,0:T(8,128)(2,1)} async-done(((bf16[96,768]{1,0:T(8,128)(2,1)}), bf16[3072,768]{1,0:T(8,128)(2,1)}) %all-gather.4.cloned.1.call-update) | async-done | bytes 4718608 | tf_op jit(solution)/shard_map/all_gather | solution.py:56
  78.0 140.4 %all-gather.6.cloned.1.call-done = bf16[1,1024,3072]{2,1,0:T(8,128)(2,1)} async-done(((bf16[1,128,3072]{2,1,0:T(8,128)(2,1)}), bf16[1,1024,3072]{2,1,0:T(8,128)(2,1)}) %all-gather.6.cloned.1.call-update) | async-done | bytes 6291472 | tf_op jit(solution)/shard_map/all_gather | solution.py:52
  218.4 8.6 %fusion.72 = bf16[1024,768]{0,1:T(8,128)(2,1)S(1)} fusion(bf16[3072,768]{1,0:T(8,128)(2,1)} %all-gather.4.cloned.1.call-done, bf16[1,1024,3072]{2,1,0:T(8,128)(2,1)} %all-gather.6.cloned.1.call-done), kind=kOutput, calls=%fused_computation.78 | convolution fusion | flops 4832624640 | bytes 12582912 | tf_op jit(solution)/shard_map/dot_general | solution.py:54
  227.0 1.1 maximum_bitcast_fusion
  228.2 0.0 copy-done.1
  228.2 0.0 copy-done.2
  228.2 12.8 %while.10 = (s32[]{:T(128)}, bf16[2,1152,3,128]{1,3,2,0:T(8,128)(2,1)S(1)}, bf16[2,1152,3,128]{1,3,2,0:T(8,128)(2,1)S(1)}, f32[128]{0:T(128)S(1)}, f32[128]{0:T(...) while((s32[]{:T(128)}, bf16[2,1152,3,128]{1,3,2,0:T(8,128)(2,1)S(1)}, ...), condition=%wide.region_7.8_spmd, body=%wide.region_0.7_spmd.sunk | while | flops 1723908096 | bytes 53539960 | solution.py:44
  228.2 0.1 dynamic-slice_bitcast_fusion.2
  228.3 0.1 fusion.95
  228.4 0.0 copy-start
  228.4 1.0 fusion.96
  229.5 0.0 copy-done
  229.5 1.0 multiply_reduce_fusion.2
  230.5 1.1 multiply_convert_fusion.2
  231.6 0.9 convolution_multiply_fusion.4
  232.5 0.7 fusion.98
  233.2 0.2 fusion.99
  233.5 0.9 fusion.97
  234.4 0.1 maximum_dynamic-update-slice_fusion.2
  234.6 0.1 dynamic-slice_bitcast_fusion.2
  234.7 0.1 fusion.95
  234.8 0.0 copy-start
  234.8 1.0 fusion.96
  235.9 0.0 copy-done
  235.9 1.0 multiply_reduce_fusion.2
  236.9 1.1 multiply_convert_fusion.2
  238.0 0.9 convolution_multiply_fusion.4
  238.9 0.7 fusion.98
  239.6 0.2 fusion.99
  239.9 0.9 fusion.97
  240.8 0.1 maximum_dynamic-update-slice_fusion.2
  241.0 0.2 slice.25
  241.2 9.5 %fusion.69 = bf16[3072,768]{0,1:T(8,128)(2,1)} fusion(bf16[1024,768]{0,1:T(8,128)(2,1)S(1)} %bitcast.149, bf16[1,1024,3072]{2,1,0:T(8,128)(2,1)} %all-gather.6.cloned.1.call-done), kind=kOutput, calls=%fused_computation.76 | convolution fusion | flops 4834197504 | bytes 12582912 | tf_op jit(solution)/shard_map/dot_general | solution.py:65
  250.7 6.6 %copy.25 = bf16[3072,768]{1,0:T(8,128)(2,1)} copy(bf16[3072,768]{0,1:T(8,128)(2,1)} %fusion.69) | data formatting | bytes 9437184
  257.3 0.0 reduce-scatter.4.cloned.1.call-update
  257.4 0.8 copy.23
  258.2 143.5 %reduce-scatter.4.cloned.1.call-done = bf16[96,768]{1,0:T(8,128)(2,1)} async-done(((bf16[3072,768]{1,0:T(8,128)(2,1)}), bf16[96,768]{1,0:T(8,128)(2,1)}) %reduce-scatter.4.cloned.1.call-update) | async-done | bytes 147472
  401.7 1.1 copy.26
  402.8 0.9 copy.22
  (8 shorter events, 0.1 us)
Async XLA Ops:
  7.2 70.9 %all-gather.4.cloned.1.call-start = ((), (), s32[]{:S(2)}) async-start(), calls=%async_computation.1 | async-start | bytes 4866048 | tf_op jit(solution)/shard_map/all_gather | solution.py:56
  7.9 210.5 %all-gather.6.cloned.1.call-start = ((), (), s32[]{:S(2)}) async-start(), calls=%async_computation.2 | async-start | bytes 7077888 | tf_op jit(solution)/shard_map/all_gather | solution.py:52
  8.6 393.0 %reduce-scatter.4.cloned.1.call-start = ((), (), s32[]{:S(2)}) async-start(), calls=%async_computation.3 | async-start | bytes 4866048
  12.6 215.6 %copy-start.1 = (f32[128]{0:T(128)S(1)}, f32[128]{0:T(128)}, u32[]{:S(2)}) copy-start(f32[128]{0:T(128)} %param.11) | copy-start | bytes 1540
  12.6 215.6 %copy-start.2 = (f32[128]{0:T(128)S(1)}, f32[128]{0:T(128)}, u32[]{:S(2)}) copy-start(f32[128]{0:T(128)} %param.12) | copy-start | bytes 1540
  228.4 1.1 copy-start
  234.8 1.1 copy-start
Sparse Core Ops, SparseCore 0:
  9.9 68.1 all-gather.3
  80.6 137.7 all-gather.5
  257.5 144.1 reduce-scatter.3
where the time goes:
time: 415 us; the launch traced here: 410 us
  waiting for transfers between devices  351 us (85%)
  matrix products  27.3 us (7%)
  between operations  13.8 us (3%)
  local copies, waits for them, and re-layouts  13.7 us (3%)
  other arithmetic  4.29 us (1%)
    unnamed x4, waiting for transfers between devices  145 us
    all_gather x1, waiting for transfers between devices, per_device(): gathered = lax.all_gather(image_rows, 'seq', axis=0, tiled=True)  140 us
    all_gather x1, waiting for transfers between devices, per_device(): lax.all_gather(w_qkv, 'dp', axis=0, tiled=True)  65.5 us
    unnamed x10, local copies, waits for them, and re-layouts  13.3 us
    dot_general x1, matrix products, per_device(): lax.dot_general(slab_part, image_grad, (((0,), (0,)), ((), ())), preferre...  9.5 us
    dot_general x1, matrix products, per_device(): jnp.dot(slab_part, lax.all_gather(w_qkv, 'dp', axis=0, tiled=True), prefe...  8.61 us
  transfers between devices with their start and end apart: 3, of which 3 were waited for; matrix products, arithmetic and copies ran while one was open for 1% of the time, Pallas kernels for 0%

commit v1 on v0

v1 whole, which is shorter than its diff:
```python
import jax
import jax.numpy as jnp
from jax import lax
from jax.experimental import pallas as pl
from jax.experimental.pallas import tpu as pltpu
from jax.sharding import PartitionSpec as P

F32, BF16 = jnp.float32, jnp.bfloat16
MESH = pl.DeviceIdType.MESH
D, HD, TXT, SEQ, IMG = 3072, 128, 128, 1152, 1024
HC = 3 * HD
SCALE = HD ** -0.5
LOG2E = 1.4426950408889634
NT = (((1,), (1,)), ((), ()))
TN = (((0,), (0,)), ((), ()))


def dot(a, b, dims=(((1,), (0,)), ((), ()))):
    return lax.dot_general(a, b, dims, preferred_element_type=F32)


def ds(start, size, align):
    return pl.ds(pl.multiple_of(start, align), size)


def project(x, w, joined, first, count, tile):
    def body(t, _):
        r = first + t * tile
        joined[ds(TXT + r, tile, 128), :] = dot(x[ds(r, tile, 128), :], w[...]).astype(BF16)
        return 0

    lax.fori_loop(0, count // tile, body, 0)


def unit_rows(rows):
    rows = rows.astype(F32)
    inverse = lax.rsqrt(jnp.mean(rows * rows, -1, keepdims=True) + 1e-6)
    return rows * inverse, inverse


def attention_start(joined, qg, kg, qn, kn, knt, dk, dv):
    qn[...] = (unit_rows(joined[:, 0:HD])[0] * qg).astype(BF16)
    keys = (unit_rows(joined[:, HD:2 * HD])[0] * kg).astype(BF16)
    kn[...] = keys
    knt[...] = keys.T
    dk[...] = jnp.zeros_like(dk)
    dv[...] = jnp.zeros_like(dv)


def attention_block(joined, dout, qn, kn, knt, dqt, dk, dv, first, count):
    cols = pl.ds(first, count)
    qb, gb = qn[cols, :], dout[cols, :]
    powers = jnp.exp2(dot(kn[...], qb, NT) * (SCALE * LOG2E))
    inverse = 1.0 / jnp.sum(powers, 0, keepdims=True)
    dp = dot(joined[:, 2 * HD:], gb, NT)
    centre = jnp.sum(powers * dp, 0, keepdims=True) * inverse
    probs = (powers * inverse).astype(BF16)
    dscore = (powers * (dp - centre) * (inverse * SCALE)).astype(BF16)
    dv[...] += dot(probs, gb)
    dk[...] += dot(dscore, qb)
    dqt[:, cols] = dot(knt[...], dscore)


def attention_end(joined, qg, kg, dqt, dk, dv, grads):
    for at, gain, grad in ((0, qg, dqt[...].T), (HD, kg, dk[...])):
        unit, inverse = unit_rows(joined[:, at:at + HD])
        grad = grad * gain
        grad = inverse * (grad - unit * jnp.mean(grad * unit, -1, keepdims=True))
        grads[:, at:at + HD] = grad.astype(BF16)
    grads[:, 2 * HD:] = dv[...].astype(BF16)


class Net:
    def __init__(self, send_sems, recv_sems):
        self.sems, self.count, self.open = (send_sems, recv_sems), 0, []

    def send(self, src, dst, device):
        i = self.count
        self.count += 1
        copy = pltpu.make_async_remote_copy(
            src_ref=src, dst_ref=dst, send_sem=self.sems[0].at[i], recv_sem=self.sems[1].at[i],
            device_id=device, device_id_type=MESH)
        copy.start()
        self.open.append(copy)
        return copy

    def finish(self):
        for copy in self.open:
            copy.wait_send()


NSEM = 96


def make_kernel(upto):
    def kernel(x_ref, t_ref, w_ref, qg_ref, kg_ref, d_ref, gw_ref, gt_ref,
               xs, wg, joined, grads, dout, qn, kn, knt, dqt, dk, dv, acc, gb,
               from_a, from_b, from_l, from_r, zs, zr, tot, sib_w, sib_t, lsem, ssem, rsem):
        dp, seq = lax.axis_index("dp"), lax.axis_index("seq")
        c, zl, y = dp % 2, (dp // 2) % 4, dp // 8
        x, zh = seq % 4, seq // 4
        s = 1 - c
        chip = y * 4 + zl

        def at(yy, zz, cc):
            return {"dp": ((yy % 4) * 4 + zz % 4) * 2 + cc, "seq": seq}

        sib = at(y, zl, s)
        x_right = {"dp": dp, "seq": zh * 4 + (x + 1) % 4}
        x_left = {"dp": dp, "seq": zh * 4 + (x + 3) % 4}
        z_far = {"dp": dp, "seq": (1 - zh) * 4 + x}
        y_right, y_left = at(y + 1, zl, c), at(y + 3, zl, c)
        z_near = [at(y, zl + k, c) for k in (1, 2, 3)]
        qg, kg = qg_ref[...], kg_ref[...]

        local = [
            pltpu.make_async_copy(x_ref, xs.at[c, ds(seq * 128, 128, 128)], lsem.at[0]),
            pltpu.make_async_copy(w_ref.at[:, ds(c * HC, HC, 128)], wg.at[ds(chip * 192 + c * 96, 96, 32)], lsem.at[1]),
            pltpu.make_async_copy(d_ref.at[:, ds(c * HD, HD, 128)], dout.at[c], lsem.at[2]),
            pltpu.make_async_copy(t_ref.at[:, ds(c * HC, HC, 128)], joined.at[c, pl.ds(0, TXT)], lsem.at[3]),
        ]
        for copy in local:
            copy.start()
        barrier = pltpu.get_barrier_semaphore()
        peers = [sib, x_right, x_left, z_far, y_right, y_left] + z_near
        for peer in peers:
            pl.semaphore_signal(barrier, inc=1, device_id=peer, device_id_type=MESH)
        pl.semaphore_wait(barrier, len(peers))
        net = Net(ssem, rsem)

        def xrows(image, slot, half, part=None):
            start = slot * 128 + half * 64
            if part is None:
                return xs.at[image, ds(start, 64, 64)]
            return xs.at[image, ds(start + part * 32, 32, 32)]

        class Ring:
            def __init__(self, image, group, source=None):
                self.image, self.base = image, group * 4
                self.mine = self.base + x
                self.left, self.right = self.base + (x + 3) % 4, self.base + (x + 1) % 4
                self.far = self.base + (x + 2) % 4
                self.source = source or (lambda part: xrows(image, self.mine, c, part))
                self.to_right, self.to_left = {}, {}

            def send(self, part, first_right):
                for right in (first_right, not first_right):
                    table, device = (self.to_right, x_right) if right else (self.to_left, x_left)
                    table[part] = net.send(self.source(part), xrows(self.image, self.mine, c, part), device)

            def forward(self):
                self.to_right[0].wait_recv()
                block = xrows(self.image, self.left, c, 0)
                self.on_right = net.send(block, block, x_right)
                self.to_left[1].wait_recv()
                block = xrows(self.image, self.right, c, 1)
                self.on_left = net.send(block, block, x_left)

            def share_near(self):
                self.to_right[1].wait_recv()
                self.to_left[0].wait_recv()
                self.shared = [share(self.image, slot) for slot in (self.left, self.right)]

            def share_far(self):
                self.on_right.wait_recv()
                self.on_left.wait_recv()
                self.shared.append(share(self.image, self.far))

            def arrived(self):
                for copy in self.shared:
                    copy.wait_recv()

        def share(image, slot):
            block = xrows(image, slot, c)
            return net.send(block, block, sib)

        w_sib = net.send(w_ref.at[:, ds(s * HC, HC, 128)], wg.at[ds(chip * 192 + c * 96, 96, 32)], sib)
        x_sib = [net.send(x_ref.at[ds(h * 64, 64, 64)], xrows(c, seq, h), sib) for h in (s, c)]
        ring_c = Ring(c, zh, lambda part: x_ref.at[ds(c * 64 + part * 32, 32, 32)])
        ring_c.send(0, True)
        ring_c.send(1, False)
        d_sib = net.send(d_ref.at[:, ds(s * HD, HD, 128)], dout.at[c], sib)
        t_sib = net.send(t_ref.at[:, ds(s * HC, HC, 128)], joined.at[c, pl.ds(0, TXT)], sib)

        local[1].wait()
        w_sib.wait_recv()
        block = wg.at[ds(chip * 192, 192, 64)]
        w_near = [net.send(block, block, peer) for peer in z_near]
        local[0].wait()
        x_sib[0].wait_recv()
        ring_s = Ring(s, zh)
        ring_s.send(0, True)
        ring_s.send(1, False)

        def z_send(image):
            return [net.send(xrows(image, seq, c, part), xrows(image, seq, c, part), z_far) for part in (0, 1)]

        def wrows(group, part):
            return wg.at[ds((group % 4) * 768 + part * 384, 384, 128)]

        if upto >= 1:
            for copy in w_near:
                copy.wait_recv()
            wr0 = net.send(wrows(y, 0), wrows(y, 0), y_right)
            wl1 = net.send(wrows(y, 1), wrows(y, 1), y_left)
            wr1 = net.send(wrows(y, 1), wrows(y, 1), y_right)
            wl0 = net.send(wrows(y, 0), wrows(y, 0), y_left)
            z0 = z_send(0)
        ring_c.forward()
        ring_s.forward()
        if upto >= 1:
            wr0.wait_recv()
            wrr = net.send(wrows(y + 3, 0), wrows(y + 3, 0), y_right)
            wl1.wait_recv()
            wll = net.send(wrows(y + 1, 1), wrows(y + 1, 1), y_left)
            ring0 = Ring(0, 1 - zh)
            ring1 = Ring(1, 1 - zh)
            z0[0].wait_recv()
            ring0.send(0, True)
            z1 = z_send(1)
            z0[1].wait_recv()
            ring0.send(1, False)
            far0 = share(0, ring0.mine)
        ring_c.share_near()
        ring_s.share_near()
        ring_c.share_far()
        ring_s.share_far()
        if upto >= 1:
            z1[0].wait_recv()
            ring1.send(0, True)
            ring0.forward()
            z1[1].wait_recv()
            ring1.send(1, False)
            far1 = share(1, ring1.mine)
            for copy in (wr1, wl0, wrr, wll):
                copy.wait_recv()
        x_sib[1].wait_recv()
        d_sib.wait_recv()
        t_sib.wait_recv()
        local[2].wait()
        local[3].wait()
        ring_c.arrived()
        ring_s.arrived()

        def attend(image, hooks):
            attention_start(joined.at[image], qg, kg, qn, kn, knt, dk, dv)
            for i, hook in enumerate(hooks):
                attention_block(joined.at[image], dout.at[image], qn, kn, knt, dqt, dk, dv,
                                i * (SEQ // len(hooks)), SEQ // len(hooks))
                if hook is not None:
                    hook()
            attention_end(joined.at[image], qg, kg, dqt, dk, dv, grads.at[image])

        if upto >= 1:
            if upto >= 2:
                project(xs.at[0], wg, joined.at[0], zh * 512, 512, 512)
            ring0.share_near()
            ring0.share_far()
            if upto >= 2:
                project(xs.at[1], wg, joined.at[1], zh * 512, 512, 512)
            far0.wait_recv()
            ring0.arrived()
            if upto >= 2:
                project(xs.at[0], wg, joined.at[0], (1 - zh) * 512, 512, 512)
            ring1.forward()
            if upto >= 3:
                attend(0, [None, ring1.share_near, None])
            else:
                ring1.share_near()
            ring1.share_far()
            if upto >= 4:
                def early(t, _):
                    cols = ds(t * 768, 768, 128)
                    acc[cols, :] = dot(xs[0, :, cols], grads[0, TXT:, :], TN)
                    return 0
                lax.fori_loop(0, 4, early, 0)
            far1.wait_recv()
            ring1.arrived()
            if upto >= 2:
                project(xs.at[1], wg, joined.at[1], (1 - zh) * 512, 512, 512)
            if upto >= 3:
                attend(1, [None, None, None])
                text = net.send(grads.at[s, pl.ds(0, TXT)], sib_t, sib)

        def late(group):
            cols = ds((group % 4) * 768, 768, 128)
            total = acc[cols, :] + dot(xs[1, :, cols], grads[1, TXT:, :], TN)
            acc[cols, :] = total
            gb[cols, :] = total.astype(BF16)

        def grows(group, part):
            return ds((group % 4) * 768 + part * 384, 384, 128)

        lo, hi = pl.ds(0, 384), pl.ds(384, 384)
        if upto >= 4:
            late(y + 2)
            if upto >= 5:
                ga = net.send(gb.at[grows(y + 2, 0)], from_a, y_right)
                gl = net.send(gb.at[grows(y + 2, 1)], from_b, y_left)
            late(y + 1)
            if upto >= 5:
                r1 = net.send(gb.at[grows(y + 1, 1)], from_l.at[hi], y_right)
            late(y + 3)
            if upto >= 5:
                l0 = net.send(gb.at[grows(y + 3, 0)], from_r.at[lo], y_left)
                ga.wait_recv()
                rows = grows(y + 1, 0)
                gb[rows, :] = (acc[rows, :] + from_a[...].astype(F32)).astype(BF16)
                r0 = net.send(gb.at[rows], from_l.at[lo], y_right)
                gl.wait_recv()
                rows = grows(y + 3, 1)
                gb[rows, :] = (acc[rows, :] + from_b[...].astype(F32)).astype(BF16)
                l1 = net.send(gb.at[rows], from_r.at[hi], y_left)
            late(y)
            if upto >= 5:
                for part, copies in ((0, (l0, r0)), (1, (r1, l1))):
                    for copy in copies:
                        copy.wait_recv()
                    rows, half = grows(y, part), pl.ds(part * 384, 384)
                    total = acc[rows, :] + from_l[half, :].astype(F32) + from_r[half, :].astype(F32)
                    acc[rows, :] = total
                    zs[half, :] = total.astype(BF16)
                gz = [net.send(zs.at[ds(((zl + k) % 4) * 192, 192, 64)], zr.at[k - 1], z_near[k - 1]) for k in (1, 2, 3)]
                for copy in gz:
                    copy.wait_recv()
                total = acc[ds(chip * 192, 192, 64), :]
                for k in range(3):
                    total = total + zr[k].astype(F32)
                tot[...] = total
                last = net.send(tot.at[ds(s * 96, 96, 32)], sib_w, sib)
                gw_ref[:, ds(c * HC, HC, 128)] = tot[ds(c * 96, 96, 32), :]
                last.wait_recv()
                gw_ref[:, ds(s * HC, HC, 128)] = sib_w[...]
        if upto >= 3:
            text.wait_recv()
            gt_ref[:, ds(c * HC, HC, 128)] = grads[c, 0:TXT, :]
            gt_ref[:, ds(s * HC, HC, 128)] = sib_t[...]
        net.finish()

    return kernel


def make_device(upto=9):
    def per_device(x_img, txt_qkv, w_qkv, q_gain, k_gain, d_out):
        hbm, vmem = pl.BlockSpec(memory_space=pl.ANY), pl.BlockSpec(memory_space=pltpu.VMEM)
        grad_w, grad_t = pl.pallas_call(
            make_kernel(upto),
            name="joint_block",
            out_shape=(jax.ShapeDtypeStruct((96, 2 * HC), F32), jax.ShapeDtypeStruct((TXT, 2 * HC), BF16)),
            in_specs=[hbm, hbm, hbm, vmem, vmem, hbm],
            out_specs=(vmem, vmem),
            scratch_shapes=[
                pltpu.VMEM((2, IMG, D), BF16),
                pltpu.VMEM((D, HC), BF16),
                pltpu.VMEM((2, SEQ, HC), BF16),
                pltpu.VMEM((2, SEQ, HC), BF16),
                pltpu.VMEM((2, SEQ, HD), BF16),
                pltpu.VMEM((SEQ, HD), BF16),
                pltpu.VMEM((SEQ, HD), BF16),
                pltpu.VMEM((HD, SEQ), BF16),
                pltpu.VMEM((HD, SEQ), F32),
                pltpu.VMEM((SEQ, HD), F32),
                pltpu.VMEM((SEQ, HD), F32),
                pltpu.VMEM((D, HC), F32),
                pltpu.VMEM((D, HC), BF16),
                pltpu.VMEM((384, HC), BF16),
                pltpu.VMEM((384, HC), BF16),
                pltpu.VMEM((768, HC), BF16),
                pltpu.VMEM((768, HC), BF16),
                pltpu.VMEM((768, HC), BF16),
                pltpu.VMEM((3, 192, HC), BF16),
                pltpu.VMEM((192, HC), F32),
                pltpu.VMEM((96, HC), F32),
                pltpu.VMEM((TXT, HC), BF16),
                pltpu.SemaphoreType.DMA((4,)),
                pltpu.SemaphoreType.DMA((NSEM,)),
                pltpu.SemaphoreType.DMA((NSEM,)),
            ],
            compiler_params=pltpu.CompilerParams(
                collective_id=0, has_side_effects=True, vmem_limit_bytes=60 * 2 ** 20),
        )(x_img[0], txt_qkv[0], w_qkv, q_gain.reshape(1, HD), k_gain.reshape(1, HD), d_out[0])
        return grad_w, grad_t[None]

    return per_device


def solution(mesh, upto=9):
    in_specs = (P("dp", "seq", None), P("dp", None, "seq"), P("dp", "seq"), P(), P(), P("dp", None, "seq"))
    out_specs = (P("dp", "seq"), P("dp", None, "seq"))
    return jax.shard_map(make_device(upto), mesh=mesh, in_specs=in_specs, out_specs=out_specs, check_vma=False)
```

time: 415 us -> 133 us (0.32); the launches traced: 410 us -> 133 us
  waiting for transfers between devices: 351 us -> 0 us
  Pallas kernels: 0 us -> 129 us
  matrix products: 27.3 us -> 0 us
  between operations: 13.8 us -> 0.65 us
  local copies, waits for them, and re-layouts: 13.7 us -> 2.41 us
  other arithmetic: 4.29 us -> 0 us
    all_gather x2 -> x0, waiting for transfers between devices: 206 us -> none  [the longest x1 140 us: per_device(): gathered = lax.all_gather(image_rows, 'seq', axis=0, tiled=True)]
    unnamed x4 -> x0, waiting for transfers between devices: 145 us -> none
    pallas_call x0 -> x1, Pallas kernels: none -> 129 us  [per_device(): pl.pallas_call(make_kernel(upto), name='joint_block', out_shape=(jax.Shap...]
    dot_general x12 -> x0, matrix products: 27.3 us -> none  [the longest x1 9.5 us: per_device(): lax.dot_general(slab_part, image_grad, (((0,), (0,)), ((), ())), preferre...]
    unnamed x10 -> x4, local copies, waits for them, and re-layouts: 13.3 us -> 2.41 us
  transfers between devices with their start and end apart: 3 -> 0, of which waited for: 3 -> 0; matrix products, arithmetic and copies ran while one was open for 1% -> 0% of each run, Pallas kernels for 0% -> 0%
where the time goes in v1:
time: 133 us
  Pallas kernels  129 us (97%)
  local copies, waits for them, and re-layouts  2.41 us (2%)
    pallas_call x1, Pallas kernels, per_device(): pl.pallas_call(make_kernel(upto), name='joint_block', out_shape=(jax.Shap...  129 us

profile of v1, /device:TPU:1, one launch (start us, length us, event | category | flops | bytes accessed | tf_op | source)
XLA Modules:
  0.0 132.6 jit_solution(3483662994216919935)
XLA Ops:
  0.6 129.5 %joint_block.1 = (f32[96,768]{1,0:T(8,128)}, bf16[128,768]{1,0:T(8,128)(2,1)}) custom-call(bf16[128,3072]{1,0:T(8,128)(2,1)} %bitcast.6, bf16[128,768]{1,0:T(8,128)(2,1)} %bitcast.8, bf16[96,768]{1,0:T(8,128)(2,1)} %w_ref.1, f32[1,128]{1,0:T(1,128)} %bitcast.10, f32[1,128]{1,0:T(1,128)} %bitcast.11, bf16[1152,256]{1,0:T(8,128)(2,1)} %bitcast.7), custom_call_target="tpu_custom_call" | custom-call | tf_op jit(solution)/shard_map/joint_block/pallas_call | solution.py:346
  130.1 0.0 copy-start
  130.1 1.7 %copy.10 = f32[96,768]{1,0:T(8,128)} copy(f32[96,768]{1,0:T(8,128)} %get-tuple-element.8) | data formatting | bytes 589824
  131.9 0.0 copy-done
  131.9 0.7 copy.11
Async XLA Ops:
  130.1 1.7 %copy-start = (bf16[128,768]{1,0:T(8,128)(2,1)S(1)}, bf16[128,768]{1,0:T(8,128)(2,1)}, u32[]{:S(2)}) copy-start(bf16[128,768]{1,0:T(8,128)(2,1)} %get-tuple-element.5) | copy-start | bytes 589828

commit v2 on v1

v2 whole, which is shorter than its diff:
```python
import jax
import jax.numpy as jnp
from jax import lax
from jax.experimental import pallas as pl
from jax.experimental.pallas import tpu as pltpu
from jax.sharding import PartitionSpec as P

F32, BF16 = jnp.float32, jnp.bfloat16
MESH = pl.DeviceIdType.MESH
D, HD, TXT, SEQ, IMG = 3072, 128, 128, 1152, 1024
HC = 3 * HD
SCALE = HD ** -0.5
LOG2E = 1.4426950408889634
NT = (((1,), (1,)), ((), ()))
TN = (((0,), (0,)), ((), ()))


def dot(a, b, dims=(((1,), (0,)), ((), ()))):
    return lax.dot_general(a, b, dims, preferred_element_type=F32)


def ds(start, size, align):
    return pl.ds(pl.multiple_of(start, align), size)


def project(x, w, joined, first, count, tile):
    def body(t, _):
        r = first + t * tile
        joined[ds(TXT + r, tile, 128), :] = dot(x[ds(r, tile, 128), :], w[...]).astype(BF16)
        return 0

    lax.fori_loop(0, count // tile, body, 0)


def unit_rows(rows):
    rows = rows.astype(F32)
    inverse = lax.rsqrt(jnp.mean(rows * rows, -1, keepdims=True) + 1e-6)
    return rows * inverse, inverse


def attention_start(joined, qg, kg, qn, kn, knt, dk, dv):
    qn[...] = (unit_rows(joined[:, 0:HD])[0] * qg).astype(BF16)
    keys = (unit_rows(joined[:, HD:2 * HD])[0] * kg).astype(BF16)
    kn[...] = keys
    knt[...] = keys.T
    dk[...] = jnp.zeros_like(dk)
    dv[...] = jnp.zeros_like(dv)


def attention_block(joined, dout, qn, kn, knt, dqt, dk, dv, first, count):
    cols = pl.ds(first, count)
    qb, gb = qn[cols, :], dout[cols, :]
    powers = jnp.exp2(dot(kn[...], qb, NT) * (SCALE * LOG2E))
    inverse = 1.0 / jnp.sum(powers, 0, keepdims=True)
    dp = dot(joined[:, 2 * HD:], gb, NT)
    centre = jnp.sum(powers * dp, 0, keepdims=True) * inverse
    probs = (powers * inverse).astype(BF16)
    dscore = (powers * (dp - centre) * (inverse * SCALE)).astype(BF16)
    dv[...] += dot(probs, gb)
    dk[...] += dot(dscore, qb)
    dqt[:, cols] = dot(knt[...], dscore)


def attention_end(joined, qg, kg, dqt, dk, dv, grads):
    for at, gain, grad in ((0, qg, dqt[...].T), (HD, kg, dk[...])):
        unit, inverse = unit_rows(joined[:, at:at + HD])
        grad = grad * gain
        grad = inverse * (grad - unit * jnp.mean(grad * unit, -1, keepdims=True))
        grads[:, at:at + HD] = grad.astype(BF16)
    grads[:, 2 * HD:] = dv[...].astype(BF16)


class Net:
    def __init__(self, send_sems, recv_sems):
        self.sems, self.count, self.open = (send_sems, recv_sems), 0, []

    def send(self, src, dst, device):
        i = self.count
        self.count += 1
        copy = pltpu.make_async_remote_copy(
            src_ref=src, dst_ref=dst, send_sem=self.sems[0].at[i], recv_sem=self.sems[1].at[i],
            device_id=device, device_id_type=MESH)
        copy.start()
        self.open.append(copy)
        return copy

    def finish(self):
        for copy in self.open:
            copy.wait_send()


PARTS = 4
PROWS = 64 // PARTS
NSEM = 122
BQ = 384


def make_kernel():
    def kernel(x_ref, t_ref, w_ref, qg_ref, kg_ref, d_ref, gw_ref, gt_ref,
               xs, wg, joined, grads, dout, qn, kn, knt, dqt, dk, dv, acc, gb,
               from_a, from_b, from_l, from_r, zs, zr, tot, sib_w, sib_t, lsem, done_sem, ssem, rsem):
        dp, seq = lax.axis_index("dp"), lax.axis_index("seq")
        c, zl, y = dp % 2, (dp // 2) % 4, dp // 8
        x, zh = seq % 4, seq // 4
        s = 1 - c
        chip = y * 4 + zl

        def at(yy, zz, cc):
            return {"dp": ((yy % 4) * 4 + zz % 4) * 2 + cc, "seq": seq}

        sib = at(y, zl, s)
        x_right = {"dp": dp, "seq": zh * 4 + (x + 1) % 4}
        x_left = {"dp": dp, "seq": zh * 4 + (x + 3) % 4}
        z_far = {"dp": dp, "seq": (1 - zh) * 4 + x}
        y_right, y_left = at(y + 1, zl, c), at(y + 3, zl, c)
        z_near = [at(y, zl + k, c) for k in (1, 2, 3)]
        qg, kg = qg_ref[...], kg_ref[...]

        local = [
            pltpu.make_async_copy(x_ref, xs.at[c, ds(seq * 128, 128, 128)], lsem.at[0]),
            pltpu.make_async_copy(w_ref.at[:, ds(c * HC, HC, 128)], wg.at[ds(chip * 192 + c * 96, 96, 32)], lsem.at[1]),
            pltpu.make_async_copy(d_ref.at[:, ds(c * HD, HD, 128)], dout.at[c], lsem.at[2]),
            pltpu.make_async_copy(t_ref.at[:, ds(c * HC, HC, 128)], joined.at[c, pl.ds(0, TXT)], lsem.at[3]),
        ]
        for copy in local:
            copy.start()
        barrier = pltpu.get_barrier_semaphore()
        peers = [sib, x_right, x_left, z_far, y_right, y_left] + z_near
        for peer in peers:
            pl.semaphore_signal(barrier, inc=1, device_id=peer, device_id_type=MESH)
        pl.semaphore_wait(barrier, len(peers))
        net = Net(ssem, rsem)

        def xrows(image, slot, half, part=None):
            start = slot * 128 + half * 64
            if part is None:
                return xs.at[image, ds(start, 64, 64)]
            return xs.at[image, ds(start + part * PROWS, PROWS, PROWS)]

        class Ring:
            def __init__(self, image, group, source=None):
                self.image = image
                slots = [group * 4 + (x + k) % 4 for k in range(4)]
                self.mine, self.right, self.far, self.left = slots
                self.source = source or (lambda part: xrows(image, self.mine, c, part))
                self.to_right, self.to_left, self.on = {}, {}, []

            def send(self, part):
                for right in (True, False) if part % 2 == 0 else (False, True):
                    table, device = (self.to_right, x_right) if right else (self.to_left, x_left)
                    table[part] = net.send(self.source(part), xrows(self.image, self.mine, c, part), device)

            def forward(self, part):
                table, slot, device = (
                    (self.to_right, self.left, x_right) if part % 2 == 0 else (self.to_left, self.right, x_left))
                table[part].wait_recv()
                block = xrows(self.image, slot, c, part)
                self.on.append(net.send(block, block, device))

            def share_near(self):
                for part in range(PARTS):
                    (self.to_left if part % 2 == 0 else self.to_right)[part].wait_recv()
                self.shared = [share(self.image, slot) for slot in (self.left, self.right)]

            def share_far(self):
                for copy in self.on:
                    copy.wait_recv()
                self.shared.append(share(self.image, self.far))

            def arrived(self):
                for copy in self.shared:
                    copy.wait_recv()

        def share(image, slot):
            block = xrows(image, slot, c)
            return net.send(block, block, sib)

        w_sib = net.send(w_ref.at[:, ds(s * HC, HC, 128)], wg.at[ds(chip * 192 + c * 96, 96, 32)], sib)
        x_sib = [net.send(x_ref.at[ds(h * 64, 64, 64)], xrows(c, seq, h), sib) for h in (s, c)]
        parts = range(PARTS)
        ring_c = Ring(c, zh, lambda part: x_ref.at[ds(c * 64 + part * PROWS, PROWS, PROWS)])
        for p in parts:
            ring_c.send(p)
        d_sib = net.send(d_ref.at[:, ds(s * HD, HD, 128)], dout.at[c], sib)
        t_sib = net.send(t_ref.at[:, ds(s * HC, HC, 128)], joined.at[c, pl.ds(0, TXT)], sib)

        y_ring = {}

        def y_send(k):
            block = wg.at[ds((y * 4 + (zl + 4 - k) % 4) * 192, 192, 64)]
            y_ring[k] = [net.send(block, block, y_right), net.send(block, block, y_left)]

        def y_forward(k):
            y_ring[k][k % 2].wait_recv()
            step, device = (3, y_right) if k % 2 == 0 else (1, y_left)
            block = wg.at[ds((((y + step) % 4) * 4 + (zl + 4 - k) % 4) * 192, 192, 64)]
            y_ring[k].append(net.send(block, block, device))

        def y_arrived(k):
            for copy in (y_ring[k][1 - k % 2], y_ring[k][2]):
                copy.wait_recv()

        local[1].wait()
        w_sib.wait_recv()
        block = wg.at[ds(chip * 192, 192, 64)]
        w_near = [net.send(block, block, peer) for peer in z_near]
        y_send(0)
        local[0].wait()
        x_sib[0].wait_recv()
        ring_s = Ring(s, zh)
        z = {}

        def z_send(u):
            if u >= 2:
                pl.semaphore_wait(done_sem.at[u - 2], 3)
            z[u] = net.send(*[xrows(u // PARTS, seq, c, u % PARTS)] * 2, z_far)

        def z_done(u):
            z[u].wait_recv()
            if u < 2 * PARTS - 2:
                for peer in z_near:
                    pl.semaphore_signal(done_sem.at[u], inc=1, device_id=peer, device_id_type=MESH)

        z_send(0)
        z_send(1)
        for p in parts:
            ring_s.send(p)
        for p in parts:
            ring_c.forward(p)
        y_forward(0)
        ring_s.forward(0)
        ring_s.forward(1)
        w_near[0].wait_recv()
        y_send(1)
        ring_s.forward(2)
        ring_s.forward(3)
        w_near[2].wait_recv()
        y_send(3)
        w_near[1].wait_recv()
        y_send(2)
        ring0, ring1 = Ring(0, 1 - zh), Ring(1, 1 - zh)

        def step(ring, part):
            z_done(ring.image * PARTS + part)
            ring.send(part)

        def slots(image, first, count):
            project(xs.at[image], wg, joined.at[image], first * 128, count * 128, count * 128)

        def start(image):
            attention_start(joined.at[image], qg, kg, qn, kn, knt, dk, dv)

        def block(image, i):
            attention_block(joined.at[image], dout.at[image], qn, kn, knt, dqt, dk, dv, i * BQ, BQ)

        def end(image):
            attention_end(joined.at[image], qg, kg, dqt, dk, dv, grads.at[image])

        def early(t):
            cols = pl.ds(t * 768, 768)
            acc[cols, :] = dot(xs[0, :, cols], grads[0, TXT:, :], TN)

        step(ring0, 0)
        step(ring0, 1)
        z_send(2)
        z_send(3)
        y_forward(1)
        ring_c.share_near()
        ring_s.share_near()
        ring0.forward(0)
        y_forward(3)
        y_forward(2)
        ring0.forward(1)
        step(ring0, 2)
        z_send(4)
        ring_c.share_far()
        ring_s.share_far()
        step(ring0, 3)
        z_send(5)
        ring0.forward(2)
        far0 = share(0, ring0.mine)
        x_sib[1].wait_recv()
        d_sib.wait_recv()
        t_sib.wait_recv()
        local[2].wait()
        local[3].wait()
        for k in range(4):
            y_arrived(k)
        ring_c.arrived()
        ring_s.arrived()
        slots(0, zh * 4, 4)
        ring0.forward(3)
        step(ring1, 0)
        z_send(6)
        slots(1, zh * 4, 4)
        ring0.share_near()
        step(ring1, 1)
        z_send(7)
        ring1.forward(0)
        ring0.share_far()
        far0.wait_recv()
        ring0.arrived()
        slots(0, (1 - zh) * 4, 4)
        start(0)
        step(ring1, 2)
        ring1.forward(1)
        block(0, 0)
        step(ring1, 3)
        far1 = share(1, ring1.mine)
        ring1.forward(2)
        block(0, 1)
        ring1.forward(3)
        ring1.share_near()
        block(0, 2)
        end(0)
        early(0)
        ring1.share_far()
        early(1)
        early(2)
        early(3)
        far1.wait_recv()
        slots(1, ring1.mine, 1)
        for copy, slot in zip(ring1.shared, (ring1.left, ring1.right, ring1.far)):
            copy.wait_recv()
            slots(1, slot, 1)
        start(1)
        for i in range(3):
            block(1, i)
        end(1)
        text = net.send(grads.at[s, pl.ds(0, TXT)], sib_t, sib)

        def late(group):
            cols = ds((group % 4) * 768, 768, 128)
            total = acc[cols, :] + dot(xs[1, :, cols], grads[1, TXT:, :], TN)
            acc[cols, :] = total
            gb[cols, :] = total.astype(BF16)

        right = [(1, 0), (1, 1), (3, 0), (0, 0)]
        left = [(2, 0), (2, 1), (3, 1), (0, 1)]

        def grows(group, piece):
            return ds((group % 4) * 768 + ((zl + piece[0]) % 4) * 192 + piece[1] * 96, 96, 32)

        class Way:
            def __init__(self, ahead, device, far, total, pieces, others):
                self.ahead, self.device, self.far, self.total = ahead, device, far, total
                self.pieces, self.others = pieces, others
                self.far_copy, self.added, self.near = {}, {}, {}

            def send_far(self, i):
                self.far_copy[i] = net.send(gb.at[grows(y + 2, self.pieces[i])], self.far.at[i], self.device)

            def send_near(self, i):
                self.near[i] = net.send(gb.at[grows(y + self.ahead, self.others[i])], self.total.at[4 + i], self.device)

            def send_added(self, i):
                self.far_copy[i].wait_recv()
                rows = grows(y + self.ahead, self.pieces[i])
                gb[rows, :] = (acc[rows, :] + self.far[i].astype(F32)).astype(BF16)
                self.added[i] = net.send(gb.at[rows], self.total.at[i], self.device)

        ways = (Way(1, y_right, from_a, from_l, right, left), Way(3, y_left, from_b, from_r, left, right))
        late(y + 2)
        for i in range(4):
            for way in ways:
                way.send_far(i)
        late(y + 1)
        late(y + 3)
        late(y)
        z_copies = []

        def complete(i):
            for way, other in (ways, ways[::-1]):
                way.added[i].wait_recv()
                other.near[i].wait_recv()
                piece = way.pieces[i]
                rows = grows(y, piece)
                total = acc[rows, :] + way.total[i].astype(F32) + other.total[4 + i].astype(F32)
                k, h = piece
                if k == 0:
                    acc[rows, :] = total
                else:
                    zs[k - 1, pl.ds(h * 96, 96), :] = total.astype(BF16)
                    z_copies.append(net.send(
                        zs.at[k - 1, pl.ds(h * 96, 96)], zr.at[k - 1, pl.ds(h * 96, 96)], z_near[k - 1]))

        for i in range(4):
            for way in ways:
                way.send_added(i)
                way.send_near(i)
            if i >= 1:
                complete(i - 1)
        complete(3)
        for copy in z_copies:
            copy.wait_recv()
        total = acc[ds(chip * 192, 192, 64), :]
        for k in range(3):
            total = total + zr[k].astype(F32)
        tot[...] = total
        last = net.send(tot.at[ds(s * 96, 96, 32)], sib_w, sib)
        gw_ref[:, ds(c * HC, HC, 128)] = tot[ds(c * 96, 96, 32), :]
        last.wait_recv()
        gw_ref[:, ds(s * HC, HC, 128)] = sib_w[...]
        text.wait_recv()
        gt_ref[:, ds(c * HC, HC, 128)] = grads[c, 0:TXT, :]
        gt_ref[:, ds(s * HC, HC, 128)] = sib_t[...]
        net.finish()

    return kernel


def make_device():
    def per_device(x_img, txt_qkv, w_qkv, q_gain, k_gain, d_out):
        hbm, vmem = pl.BlockSpec(memory_space=pl.ANY), pl.BlockSpec(memory_space=pltpu.VMEM)
        grad_w, grad_t = pl.pallas_call(
            make_kernel(),
            name="joint_block",
            out_shape=(jax.ShapeDtypeStruct((96, 2 * HC), F32), jax.ShapeDtypeStruct((TXT, 2 * HC), BF16)),
            in_specs=[hbm, hbm, hbm, vmem, vmem, hbm],
            out_specs=(vmem, vmem),
            scratch_shapes=[
                pltpu.VMEM((2, IMG, D), BF16),
                pltpu.VMEM((D, HC), BF16),
                pltpu.VMEM((2, SEQ, HC), BF16),
                pltpu.VMEM((2, SEQ, HC), BF16),
                pltpu.VMEM((2, SEQ, HD), BF16),
                pltpu.VMEM((SEQ, HD), BF16),
                pltpu.VMEM((SEQ, HD), BF16),
                pltpu.VMEM((HD, SEQ), BF16),
                pltpu.VMEM((HD, SEQ), F32),
                pltpu.VMEM((SEQ, HD), F32),
                pltpu.VMEM((SEQ, HD), F32),
                pltpu.VMEM((D, HC), F32),
                pltpu.VMEM((D, HC), BF16),
                pltpu.VMEM((4, 96, HC), BF16),
                pltpu.VMEM((4, 96, HC), BF16),
                pltpu.VMEM((8, 96, HC), BF16),
                pltpu.VMEM((8, 96, HC), BF16),
                pltpu.VMEM((3, 192, HC), BF16),
                pltpu.VMEM((3, 192, HC), BF16),
                pltpu.VMEM((192, HC), F32),
                pltpu.VMEM((96, HC), F32),
                pltpu.VMEM((TXT, HC), BF16),
                pltpu.SemaphoreType.DMA((4,)),
                pltpu.SemaphoreType.REGULAR((2 * PARTS - 2,)),
                pltpu.SemaphoreType.DMA((NSEM,)),
                pltpu.SemaphoreType.DMA((NSEM,)),
            ],
            compiler_params=pltpu.CompilerParams(
                collective_id=0, has_side_effects=True, vmem_limit_bytes=60 * 2 ** 20),
        )(x_img[0], txt_qkv[0], w_qkv, q_gain.reshape(1, HD), k_gain.reshape(1, HD), d_out[0])
        return grad_w, grad_t[None]

    return per_device


def solution(mesh):
    in_specs = (P("dp", "seq", None), P("dp", None, "seq"), P("dp", "seq"), P(), P(), P("dp", None, "seq"))
    out_specs = (P("dp", "seq"), P("dp", None, "seq"))
    return jax.shard_map(make_device(), mesh=mesh, in_specs=in_specs, out_specs=out_specs, check_vma=False)
```

time: 133 us -> 121 us (0.910)
  Pallas kernels: 129 us -> 118 us
    pallas_call x1, Pallas kernels: 129 us -> 118 us  [per_device(): pl.pallas_call(make_kernel(), name='joint_block', out_shape=(jax.ShapeDty...]
where the time goes in v2:
time: 121 us
  Pallas kernels  118 us (98%)
  local copies, waits for them, and re-layouts  2.41 us (2%)
    pallas_call x1, Pallas kernels, per_device(): pl.pallas_call(make_kernel(), name='joint_block', out_shape=(jax.ShapeDty...  118 us

profile of v2, /device:TPU:1, one launch (start us, length us, event | category | flops | bytes accessed | tf_op | source)
XLA Modules:
  0.0 121.2 jit_solution(6082377298496417216)
XLA Ops:
  0.6 118.1 %joint_block.1 = (f32[96,768]{1,0:T(8,128)}, bf16[128,768]{1,0:T(8,128)(2,1)}) custom-call(bf16[128,3072]{1,0:T(8,128)(2,1)} %bitcast.6, bf16[128,768]{1,0:T(8,128)(2,1)} %bitcast.8, bf16[96,768]{1,0:T(8,128)(2,1)} %w_ref.1, f32[1,128]{1,0:T(1,128)} %bitcast.10, f32[1,128]{1,0:T(1,128)} %bitcast.11, bf16[1152,256]{1,0:T(8,128)(2,1)} %bitcast.7), custom_call_target="tpu_custom_call" | custom-call | tf_op jit(solution)/shard_map/joint_block/pallas_call | solution.py:415
  118.7 0.0 copy-start
  118.8 1.7 %copy.10 = f32[96,768]{1,0:T(8,128)} copy(f32[96,768]{1,0:T(8,128)} %get-tuple-element.8) | data formatting | bytes 589824
  120.5 0.0 copy-done
  120.5 0.7 copy.11
Async XLA Ops:
  118.7 1.7 %copy-start = (bf16[128,768]{1,0:T(8,128)(2,1)S(1)}, bf16[128,768]{1,0:T(8,128)(2,1)}, u32[]{:S(2)}) copy-start(bf16[128,768]{1,0:T(8,128)(2,1)} %get-tuple-element.5) | copy-start | bytes 589828

commit v3 on v2

--- a/solution.py
+++ b/solution.py
@@ -71,27 +71,34 @@
 
 
 class Net:
-    def __init__(self, send_sems, recv_sems):
-        self.sems, self.count, self.open = (send_sems, recv_sems), 0, []
-
-    def send(self, src, dst, device):
-        i = self.count
+    def __init__(self, send_sems, recv_sems, device):
+        self.sems, self.device = (send_sems, recv_sems), device
+        self.count, self.groups = 0, {}
+
+    def copy(self, src, dst, send, recv, device):
+        return pltpu.make_async_remote_copy(
+            src_ref=src, dst_ref=dst, send_sem=self.sems[0].at[send], recv_sem=self.sems[1].at[recv],
+            device_id=device, device_id_type=MESH)
+
+    def send(self, src, dst, device, like=None):
+        key = len(self.groups) if like is None else id(like)
+        index, rows, _ = self.groups.get(key, (len(self.groups), 0, None))
+        self.groups[key] = (index, rows + src.shape[0], src if like is None else like)
+        copy = self.copy(src, dst, index, self.count, device)
         self.count += 1
-        copy = pltpu.make_async_remote_copy(
-            src_ref=src, dst_ref=dst, send_sem=self.sems[0].at[i], recv_sem=self.sems[1].at[i],
-            device_id=device, device_id_type=MESH)
         copy.start()
-        self.open.append(copy)
         return copy
 
     def finish(self):
-        for copy in self.open:
-            copy.wait_send()
+        for index, rows, ref in self.groups.values():
+            ref = ref.at[pl.ds(0, rows)]
+            self.copy(ref, ref, index, 0, self.device).wait_send()
 
 
 PARTS = 4
 PROWS = 64 // PARTS
 NSEM = 122
+NSEND = 16
 BQ = 384
 
 
@@ -129,7 +136,9 @@
         for peer in peers:
             pl.semaphore_signal(barrier, inc=1, device_id=peer, device_id_type=MESH)
         pl.semaphore_wait(barrier, len(peers))
-        net = Net(ssem, rsem)
+        net = Net(ssem, rsem, sib)
+        x_like, w_like, g_like = xs.at[0], wg.at[:], gb.at[:]
+        z_like, n_like, s_like, q_like = xs.at[0], wg.at[:], xs.at[0], gb.at[:]
 
         def xrows(image, slot, half, part=None):
             start = slot * 128 + half * 64
@@ -138,24 +147,24 @@
             return xs.at[image, ds(start + part * PROWS, PROWS, PROWS)]
 
         class Ring:
-            def __init__(self, image, group, source=None):
+            def __init__(self, image, group):
                 self.image = image
                 slots = [group * 4 + (x + k) % 4 for k in range(4)]
                 self.mine, self.right, self.far, self.left = slots
-                self.source = source or (lambda part: xrows(image, self.mine, c, part))
                 self.to_right, self.to_left, self.on = {}, {}, []
 
             def send(self, part):
                 for right in (True, False) if part % 2 == 0 else (False, True):
                     table, device = (self.to_right, x_right) if right else (self.to_left, x_left)
-                    table[part] = net.send(self.source(part), xrows(self.image, self.mine, c, part), device)
+                    block = xrows(self.image, self.mine, c, part)
+                    table[part] = net.send(block, block, device, x_like)
 
             def forward(self, part):
                 table, slot, device = (
                     (self.to_right, self.left, x_right) if part % 2 == 0 else (self.to_left, self.right, x_left))
                 table[part].wait_recv()
                 block = xrows(self.image, slot, c, part)
-                self.on.append(net.send(block, block, device))
+                self.on.append(net.send(block, block, device, x_like))
 
             def share_near(self):
                 for part in range(PARTS):
@@ -173,14 +182,11 @@
 
         def share(image, slot):
             block = xrows(image, slot, c)
-            return net.send(block, block, sib)
+            return net.send(block, block, sib, s_like)
 
         w_sib = net.send(w_ref.at[:, ds(s * HC, HC, 128)], wg.at[ds(chip * 192 + c * 96, 96, 32)], sib)
         x_sib = [net.send(x_ref.at[ds(h * 64, 64, 64)], xrows(c, seq, h), sib) for h in (s, c)]
         parts = range(PARTS)
-        ring_c = Ring(c, zh, lambda part: x_ref.at[ds(c * 64 + part * PROWS, PROWS, PROWS)])
-        for p in parts:
-            ring_c.send(p)
         d_sib = net.send(d_ref.at[:, ds(s * HD, HD, 128)], dout.at[c], sib)
         t_sib = net.send(t_ref.at[:, ds(s * HC, HC, 128)], joined.at[c, pl.ds(0, TXT)], sib)
 
@@ -188,61 +194,81 @@
 
         def y_send(k):
             block = wg.at[ds((y * 4 + (zl + 4 - k) % 4) * 192, 192, 64)]
-            y_ring[k] = [net.send(block, block, y_right), net.send(block, block, y_left)]
+            y_ring[k] = [net.send(block, block, device, w_like) for device in (y_right, y_left)]
 
         def y_forward(k):
             y_ring[k][k % 2].wait_recv()
             step, device = (3, y_right) if k % 2 == 0 else (1, y_left)
             block = wg.at[ds((((y + step) % 4) * 4 + (zl + 4 - k) % 4) * 192, 192, 64)]
-            y_ring[k].append(net.send(block, block, device))
+            y_ring[k].append(net.send(block, block, device, w_like))
 
         def y_arrived(k):
             for copy in (y_ring[k][1 - k % 2], y_ring[k][2]):
                 copy.wait_recv()
 
+        z = {}
+
+        def z_send(u):
+            block = xrows(u // PARTS, seq, c, u % PARTS)
+            z[u] = net.send(block, block, z_far, z_like)
+
+        def step(ring, part):
+            z[ring.image * PARTS + part].wait_recv()
+            ring.send(part)
+
+        local[0].wait()
+        x_sib[0].wait_recv()
+        own0, own1, ring0, ring1 = Ring(0, zh), Ring(1, zh), Ring(0, 1 - zh), Ring(1, 1 - zh)
+        z_send(0)
+        for p in parts:
+            own0.send(p)
         local[1].wait()
         w_sib.wait_recv()
         block = wg.at[ds(chip * 192, 192, 64)]
-        w_near = [net.send(block, block, peer) for peer in z_near]
+        w_near = [net.send(block, block, peer, n_like) for peer in z_near]
+        for p in (1, 2, 3):
+            z_send(p)
         y_send(0)
-        local[0].wait()
-        x_sib[0].wait_recv()
-        ring_s = Ring(s, zh)
-        z = {}
-
-        def z_send(u):
-            if u >= 2:
-                pl.semaphore_wait(done_sem.at[u - 2], 3)
-            z[u] = net.send(*[xrows(u // PARTS, seq, c, u % PARTS)] * 2, z_far)
-
-        def z_done(u):
-            z[u].wait_recv()
-            if u < 2 * PARTS - 2:
-                for peer in z_near:
-                    pl.semaphore_signal(done_sem.at[u], inc=1, device_id=peer, device_id_type=MESH)
-
-        z_send(0)
-        z_send(1)
+        own0.forward(0)
+        own0.forward(1)
+        step(ring0, 0)
+        own0.forward(2)
+        own0.forward(3)
+        y_forward(0)
         for p in parts:
-            ring_s.send(p)
-        for p in parts:
-            ring_c.forward(p)
-        y_forward(0)
-        ring_s.forward(0)
-        ring_s.forward(1)
+            own1.send(p)
+        own0.share_near()
+        step(ring0, 1)
+        own0.share_far()
+        step(ring0, 2)
+        ring0.forward(0)
         w_near[0].wait_recv()
         y_send(1)
-        ring_s.forward(2)
-        ring_s.forward(3)
         w_near[2].wait_recv()
         y_send(3)
+        step(ring0, 3)
+        ring0.forward(1)
         w_near[1].wait_recv()
         y_send(2)
-        ring0, ring1 = Ring(0, 1 - zh), Ring(1, 1 - zh)
-
-        def step(ring, part):
-            z_done(ring.image * PARTS + part)
-            ring.send(part)
+        for peer in z_near:
+            pl.semaphore_signal(done_sem, inc=1, device_id=peer, device_id_type=MESH)
+        pl.semaphore_wait(done_sem, 3)
+        for p in parts:
+            z_send(PARTS + p)
+        far0 = share(0, ring0.mine)
+        own1.forward(0)
+        ring0.forward(2)
+        own1.forward(1)
+        y_forward(1)
+        ring0.forward(3)
+        y_forward(3)
+        own1.forward(2)
+        y_forward(2)
+        ring0.share_near()
+        own1.forward(3)
+        ring0.share_far()
+        step(ring1, 0)
+        step(ring1, 1)
 
         def slots(image, first, count):
             project(xs.at[image], wg, joined.at[image], first * 128, count * 128, count * 128)
@@ -256,29 +282,10 @@
         def end(image):
             attention_end(joined.at[image], qg, kg, dqt, dk, dv, grads.at[image])
 
-        def early(t):
-            cols = pl.ds(t * 768, 768)
+        def early(group):
+            cols = ds((group % 4) * 768, 768, 128)
             acc[cols, :] = dot(xs[0, :, cols], grads[0, TXT:, :], TN)
 
-        step(ring0, 0)
-        step(ring0, 1)
-        z_send(2)
-        z_send(3)
-        y_forward(1)
-        ring_c.share_near()
-        ring_s.share_near()
-        ring0.forward(0)
-        y_forward(3)
-        y_forward(2)
-        ring0.forward(1)
-        step(ring0, 2)
-        z_send(4)
-        ring_c.share_far()
-        ring_s.share_far()
-        step(ring0, 3)
-        z_send(5)
-        ring0.forward(2)
-        far0 = share(0, ring0.mine)
         x_sib[1].wait_recv()
         d_sib.wait_recv()
         t_sib.wait_recv()
@@ -286,38 +293,30 @@
         local[3].wait()
         for k in range(4):
             y_arrived(k)
-        ring_c.arrived()
-        ring_s.arrived()
+        own0.arrived()
         slots(0, zh * 4, 4)
-        ring0.forward(3)
-        step(ring1, 0)
-        z_send(6)
-        slots(1, zh * 4, 4)
-        ring0.share_near()
-        step(ring1, 1)
-        z_send(7)
-        ring1.forward(0)
-        ring0.share_far()
+        own1.share_near()
+        step(ring1, 2)
         far0.wait_recv()
         ring0.arrived()
         slots(0, (1 - zh) * 4, 4)
+        step(ring1, 3)
+        own1.share_far()
         start(0)
-        step(ring1, 2)
+        ring1.forward(0)
+        block(0, 0)
         ring1.forward(1)
-        block(0, 0)
-        step(ring1, 3)
+        block(0, 1)
+        ring1.forward(2)
         far1 = share(1, ring1.mine)
-        ring1.forward(2)
-        block(0, 1)
+        block(0, 2)
         ring1.forward(3)
+        end(0)
+        own1.arrived()
+        slots(1, zh * 4, 4)
         ring1.share_near()
-        block(0, 2)
-        end(0)
-        early(0)
+        early(y + 2)
         ring1.share_far()
-        early(1)
-        early(2)
-        early(3)
         far1.wait_recv()
         slots(1, ring1.mine, 1)
         for copy, slot in zip(ring1.shared, (ring1.left, ring1.right, ring1.far)):
@@ -348,25 +347,25 @@
                 self.far_copy, self.added, self.near = {}, {}, {}
 
             def send_far(self, i):
-                self.far_copy[i] = net.send(gb.at[grows(y + 2, self.pieces[i])], self.far.at[i], self.device)
+                self.far_copy[i] = net.send(gb.at[grows(y + 2, self.pieces[i])], self.far.at[i], self.device, g_like)
 
             def send_near(self, i):
-                self.near[i] = net.send(gb.at[grows(y + self.ahead, self.others[i])], self.total.at[4 + i], self.device)
+                self.near[i] = net.send(gb.at[grows(y + self.ahead, self.others[i])], self.total.at[4 + i], self.device, g_like)
 
             def send_added(self, i):
                 self.far_copy[i].wait_recv()
                 rows = grows(y + self.ahead, self.pieces[i])
                 gb[rows, :] = (acc[rows, :] + self.far[i].astype(F32)).astype(BF16)
-                self.added[i] = net.send(gb.at[rows], self.total.at[i], self.device)
+                self.added[i] = net.send(gb.at[rows], self.total.at[i], self.device, g_like)
 
         ways = (Way(1, y_right, from_a, from_l, right, left), Way(3, y_left, from_b, from_r, left, right))
         late(y + 2)
         for i in range(4):
             for way in ways:
                 way.send_far(i)
-        late(y + 1)
-        late(y + 3)
-        late(y)
+        for step_y in (1, 3, 0):
+            early(y + step_y)
+            late(y + step_y)
         z_copies = []
 
         def complete(i):
@@ -382,7 +381,7 @@
                 else:
                     zs[k - 1, pl.ds(h * 96, 96), :] = total.astype(BF16)
                     z_copies.append(net.send(
-                        zs.at[k - 1, pl.ds(h * 96, 96)], zr.at[k - 1, pl.ds(h * 96, 96)], z_near[k - 1]))
+                        zs.at[k - 1, pl.ds(h * 96, 96)], zr.at[k - 1, pl.ds(h * 96, 96)], z_near[k - 1], q_like))
 
         for i in range(4):
             for way in ways:
@@ -442,8 +441,8 @@
                 pltpu.VMEM((96, HC), F32),
                 pltpu.VMEM((TXT, HC), BF16),
                 pltpu.SemaphoreType.DMA((4,)),
-                pltpu.SemaphoreType.REGULAR((2 * PARTS - 2,)),
-                pltpu.SemaphoreType.DMA((NSEM,)),
+                pltpu.SemaphoreType.REGULAR,
+                pltpu.SemaphoreType.DMA((NSEND,)),
                 pltpu.SemaphoreType.DMA((NSEM,)),
             ],
             compiler_params=pltpu.CompilerParams(

time: 121 us -> 114 us (0.942)
  Pallas kernels: 118 us -> 111 us
    pallas_call x1, Pallas kernels: 118 us -> 111 us  [per_device(): pl.pallas_call(make_kernel(), name='joint_block', out_shape=(jax.ShapeDty...]
where the time goes in v3:
time: 114 us
  Pallas kernels  111 us (97%)
  local copies, waits for them, and re-layouts  2.41 us (2%)
    pallas_call x1, Pallas kernels, per_device(): pl.pallas_call(make_kernel(), name='joint_block', out_shape=(jax.ShapeDty...  111 us
    unnamed x4, local copies, waits for them, and re-layouts  2.41 us

profile of v3, /device:TPU:1, one launch (start us, length us, event | category | flops | bytes accessed | tf_op | source)
XLA Modules:
  0.0 113.9 jit_solution(16722396654903715686)
XLA Ops:
  0.6 110.9 %joint_block.1 = (f32[96,768]{1,0:T(8,128)}, bf16[128,768]{1,0:T(8,128)(2,1)}) custom-call(bf16[128,3072]{1,0:T(8,128)(2,1)} %bitcast.6, bf16[128,768]{1,0:T(8,128)(2,1)} %bitcast.8, bf16[96,768]{1,0:T(8,128)(2,1)} %w_ref.1, f32[1,128]{1,0:T(1,128)} %bitcast.10, f32[1,128]{1,0:T(1,128)} %bitcast.11, bf16[1152,256]{1,0:T(8,128)(2,1)} %bitcast.7), custom_call_target="tpu_custom_call" | custom-call | tf_op jit(solution)/shard_map/joint_block/pallas_call | solution.py:414
  111.5 0.0 copy-start
  111.5 1.7 %copy.10 = f32[96,768]{1,0:T(8,128)} copy(f32[96,768]{1,0:T(8,128)} %get-tuple-element.8) | data formatting | bytes 589824
  113.2 0.0 copy-done
  113.2 0.7 copy.11
Async XLA Ops:
  111.5 1.7 %copy-start = (bf16[128,768]{1,0:T(8,128)(2,1)S(1)}, bf16[128,768]{1,0:T(8,128)(2,1)}, u32[]{:S(2)}) copy-start(bf16[128,768]{1,0:T(8,128)(2,1)} %get-tuple-element.5) | copy-start | bytes 589828

commit v4 on v3

--- a/solution.py
+++ b/solution.py
@@ -38,13 +38,11 @@
     return rows * inverse, inverse
 
 
-def attention_start(joined, qg, kg, qn, kn, knt, dk, dv):
+def attention_start(joined, qg, kg, qn, kn, knt):
     qn[...] = (unit_rows(joined[:, 0:HD])[0] * qg).astype(BF16)
     keys = (unit_rows(joined[:, HD:2 * HD])[0] * kg).astype(BF16)
     kn[...] = keys
     knt[...] = keys.T
-    dk[...] = jnp.zeros_like(dk)
-    dv[...] = jnp.zeros_like(dv)
 
 
 def attention_block(joined, dout, qn, kn, knt, dqt, dk, dv, first, count):
@@ -56,8 +54,12 @@
     centre = jnp.sum(powers * dp, 0, keepdims=True) * inverse
     probs = (powers * inverse).astype(BF16)
     dscore = (powers * (dp - centre) * (inverse * SCALE)).astype(BF16)
-    dv[...] += dot(probs, gb)
-    dk[...] += dot(dscore, qb)
+    if first == 0:
+        dv[...] = dot(probs, gb)
+        dk[...] = dot(dscore, qb)
+    else:
+        dv[...] += dot(probs, gb)
+        dk[...] += dot(dscore, qb)
     dqt[:, cols] = dot(knt[...], dscore)
 
 
@@ -76,28 +78,34 @@
         self.count, self.groups = 0, {}
 
     def copy(self, src, dst, send, recv, device):
+        recv = self.sems[1].at[recv] if isinstance(recv, int) else recv
         return pltpu.make_async_remote_copy(
-            src_ref=src, dst_ref=dst, send_sem=self.sems[0].at[send], recv_sem=self.sems[1].at[recv],
+            src_ref=src, dst_ref=dst, send_sem=self.sems[0].at[send], recv_sem=recv,
             device_id=device, device_id_type=MESH)
 
-    def send(self, src, dst, device, like=None):
+    def send(self, src, dst, device, like=None, recv=None):
         key = len(self.groups) if like is None else id(like)
         index, rows, _ = self.groups.get(key, (len(self.groups), 0, None))
         self.groups[key] = (index, rows + src.shape[0], src if like is None else like)
-        copy = self.copy(src, dst, index, self.count, device)
-        self.count += 1
+        copy = self.copy(src, dst, index, self.count if recv is None else recv, device)
+        copy.key = key
+        self.count += recv is None
         copy.start()
         return copy
 
+    def sent(self, copy):
+        copy.wait_send()
+        self.groups[copy.key] = None
+
     def finish(self):
-        for index, rows, ref in self.groups.values():
+        for index, rows, ref in filter(None, self.groups.values()):
             ref = ref.at[pl.ds(0, rows)]
             self.copy(ref, ref, index, 0, self.device).wait_send()
 
 
 PARTS = 4
 PROWS = 64 // PARTS
-NSEM = 122
+NSEM = 116
 NSEND = 16
 BQ = 384
 
@@ -105,7 +113,7 @@
 def make_kernel():
     def kernel(x_ref, t_ref, w_ref, qg_ref, kg_ref, d_ref, gw_ref, gt_ref,
                xs, wg, joined, grads, dout, qn, kn, knt, dqt, dk, dv, acc, gb,
-               from_a, from_b, from_l, from_r, zs, zr, tot, sib_w, sib_t, lsem, done_sem, ssem, rsem):
+               from_a, from_b, from_l, from_r, zs, zr, swap, sib_w, sib_t, z_sem, lsem, done_sem, ssem, rsem):
         dp, seq = lax.axis_index("dp"), lax.axis_index("seq")
         c, zl, y = dp % 2, (dp // 2) % 4, dp // 8
         x, zh = seq % 4, seq // 4
@@ -132,7 +140,8 @@
         for copy in local:
             copy.start()
         barrier = pltpu.get_barrier_semaphore()
-        peers = [sib, x_right, x_left, z_far, y_right, y_left] + z_near
+        z_cross = [at(y, zl + k, s) for k in (1, 2, 3)]
+        peers = [sib, x_right, x_left, z_far, y_right, y_left] + z_near + z_cross
         for peer in peers:
             pl.semaphore_signal(barrier, inc=1, device_id=peer, device_id_type=MESH)
         pl.semaphore_wait(barrier, len(peers))
@@ -210,7 +219,7 @@
 
         def z_send(u):
             block = xrows(u // PARTS, seq, c, u % PARTS)
-            z[u] = net.send(block, block, z_far, z_like)
+            z[u] = net.send(block, block, z_far, None if u in (4, 5) else z_like)
 
         def step(ring, part):
             z[ring.image * PARTS + part].wait_recv()
@@ -253,8 +262,8 @@
         for peer in z_near:
             pl.semaphore_signal(done_sem, inc=1, device_id=peer, device_id_type=MESH)
         pl.semaphore_wait(done_sem, 3)
-        for p in parts:
-            z_send(PARTS + p)
+        z_send(4)
+        z_send(5)
         far0 = share(0, ring0.mine)
         own1.forward(0)
         ring0.forward(2)
@@ -266,15 +275,19 @@
         y_forward(2)
         ring0.share_near()
         own1.forward(3)
-        ring0.share_far()
+        net.sent(z[4])
+        z_send(6)
+        net.sent(z[5])
+        z_send(7)
         step(ring1, 0)
         step(ring1, 1)
+        ring0.share_far()
 
         def slots(image, first, count):
             project(xs.at[image], wg, joined.at[image], first * 128, count * 128, count * 128)
 
         def start(image):
-            attention_start(joined.at[image], qg, kg, qn, kn, knt, dk, dv)
+            attention_start(joined.at[image], qg, kg, qn, kn, knt)
 
         def block(image, i):
             attention_block(joined.at[image], dout.at[image], qn, kn, knt, dqt, dk, dv, i * BQ, BQ)
@@ -366,8 +379,6 @@
         for step_y in (1, 3, 0):
             early(y + step_y)
             late(y + step_y)
-        z_copies = []
-
         def complete(i):
             for way, other in (ways, ways[::-1]):
                 way.added[i].wait_recv()
@@ -379,9 +390,9 @@
                 if k == 0:
                     acc[rows, :] = total
                 else:
-                    zs[k - 1, pl.ds(h * 96, 96), :] = total.astype(BF16)
-                    z_copies.append(net.send(
-                        zs.at[k - 1, pl.ds(h * 96, 96)], zr.at[k - 1, pl.ds(h * 96, 96)], z_near[k - 1], q_like))
+                    piece = pl.ds(h * 96, 96)
+                    zs[k - 1, piece, :] = total.astype(BF16)
+                    net.send(zs.at[k - 1, piece], zr.at[c, k - 1], at(y, zl + k, h), q_like, z_sem.at[k - 1, c])
 
         for i in range(4):
             for way in ways:
@@ -390,16 +401,20 @@
             if i >= 1:
                 complete(i - 1)
         complete(3)
-        for copy in z_copies:
-            copy.wait_recv()
-        total = acc[ds(chip * 192, 192, 64), :]
+        swap[...] = acc[ds(chip * 192 + s * 96, 96, 32), :].astype(BF16)
+        last = net.send(swap, sib_w, sib)
         for k in range(3):
-            total = total + zr[k].astype(F32)
-        tot[...] = total
-        last = net.send(tot.at[ds(s * 96, 96, 32)], sib_w, sib)
-        gw_ref[:, ds(c * HC, HC, 128)] = tot[ds(c * 96, 96, 32), :]
+            for core in range(2):
+                net.copy(zr.at[core, k], zr.at[core, k], 0, z_sem.at[k, core], sib).wait_recv()
+        total = acc[ds(chip * 192 + c * 96, 96, 32), :]
+        for k in range(3):
+            total = total + zr[c, k].astype(F32)
+        gw_ref[:, ds(c * HC, HC, 128)] = total
         last.wait_recv()
-        gw_ref[:, ds(s * HC, HC, 128)] = sib_w[...]
+        total = sib_w[...].astype(F32)
+        for k in range(3):
+            total = total + zr[s, k].astype(F32)
+        gw_ref[:, ds(s * HC, HC, 128)] = total
         text.wait_recv()
         gt_ref[:, ds(c * HC, HC, 128)] = grads[c, 0:TXT, :]
         gt_ref[:, ds(s * HC, HC, 128)] = sib_t[...]
@@ -436,10 +451,11 @@
                 pltpu.VMEM((8, 96, HC), BF16),
                 pltpu.VMEM((8, 96, HC), BF16),
                 pltpu.VMEM((3, 192, HC), BF16),
-                pltpu.VMEM((3, 192, HC), BF16),
-                pltpu.VMEM((192, HC), F32),
-                pltpu.VMEM((96, HC), F32),
+                pltpu.VMEM((2, 3, 96, HC), BF16),
+                pltpu.VMEM((96, HC), BF16),
+                pltpu.VMEM((96, HC), BF16),
                 pltpu.VMEM((TXT, HC), BF16),
+                pltpu.SemaphoreType.DMA((3, 2)),
                 pltpu.SemaphoreType.DMA((4,)),
                 pltpu.SemaphoreType.REGULAR,
                 pltpu.SemaphoreType.DMA((NSEND,)),

time: 114 us -> 112 us (0.982)
  Pallas kernels: 111 us -> 109 us
    pallas_call x1, Pallas kernels: 111 us -> 109 us  [per_device(): pl.pallas_call(make_kernel(), name='joint_block', out_shape=(jax.ShapeDty...]
where the time goes in v4:
time: 112 us
  Pallas kernels  109 us (97%)
  local copies, waits for them, and re-layouts  2.41 us (2%)
    pallas_call x1, Pallas kernels, per_device(): pl.pallas_call(make_kernel(), name='joint_block', out_shape=(jax.ShapeDty...  109 us
    unnamed x4, local copies, waits for them, and re-layouts  2.41 us

profile of v4, /device:TPU:1, one launch (start us, length us, event | category | flops | bytes accessed | tf_op | source)
XLA Modules:
  0.0 112.3 jit_solution(16533489529633105300)
XLA Ops:
  0.6 109.2 %joint_block.1 = (f32[96,768]{1,0:T(8,128)}, bf16[128,768]{1,0:T(8,128)(2,1)}) custom-call(bf16[128,3072]{1,0:T(8,128)(2,1)} %bitcast.6, bf16[128,768]{1,0:T(8,128)(2,1)} %bitcast.8, bf16[96,768]{1,0:T(8,128)(2,1)} %w_ref.1, f32[1,128]{1,0:T(1,128)} %bitcast.10, f32[1,128]{1,0:T(1,128)} %bitcast.11, bf16[1152,256]{1,0:T(8,128)(2,1)} %bitcast.7), custom_call_target="tpu_custom_call" | custom-call | tf_op jit(solution)/shard_map/joint_block/pallas_call | solution.py:429
  109.8 0.0 copy-start
  109.8 1.7 %copy.10 = f32[96,768]{1,0:T(8,128)} copy(f32[96,768]{1,0:T(8,128)} %get-tuple-element.8) | data formatting | bytes 589824
  111.6 0.0 copy-done
  111.6 0.7 copy.11
Async XLA Ops:
  109.8 1.7 %copy-start = (bf16[128,768]{1,0:T(8,128)(2,1)S(1)}, bf16[128,768]{1,0:T(8,128)(2,1)}, u32[]{:S(2)}) copy-start(bf16[128,768]{1,0:T(8,128)(2,1)} %get-tuple-element.5) | copy-start | bytes 589828

commit v5 on v4

--- a/solution.py
+++ b/solution.py
@@ -156,17 +156,17 @@
             return xs.at[image, ds(start + part * PROWS, PROWS, PROWS)]
 
         class Ring:
-            def __init__(self, image, group):
-                self.image = image
+            def __init__(self, image, group, parts):
+                self.image, self.parts = image, parts
                 slots = [group * 4 + (x + k) % 4 for k in range(4)]
                 self.mine, self.right, self.far, self.left = slots
                 self.to_right, self.to_left, self.on = {}, {}, []
 
-            def send(self, part):
+            def send(self, part, source=None):
                 for right in (True, False) if part % 2 == 0 else (False, True):
                     table, device = (self.to_right, x_right) if right else (self.to_left, x_left)
                     block = xrows(self.image, self.mine, c, part)
-                    table[part] = net.send(block, block, device, x_like)
+                    table[part] = net.send(source or block, block, device, x_like)
 
             def forward(self, part):
                 table, slot, device = (
@@ -175,14 +175,20 @@
                 block = xrows(self.image, slot, c, part)
                 self.on.append(net.send(block, block, device, x_like))
 
-            def share_near(self):
-                for part in range(PARTS):
+            def near_wait(self):
+                for part in self.parts:
                     (self.to_left if part % 2 == 0 else self.to_right)[part].wait_recv()
-                self.shared = [share(self.image, slot) for slot in (self.left, self.right)]
-
-            def share_far(self):
+
+            def far_wait(self):
                 for copy in self.on:
                     copy.wait_recv()
+
+            def share_near(self):
+                self.near_wait()
+                self.shared = [share(self.image, slot) for slot in (self.left, self.right)]
+
+            def share_far(self):
+                self.far_wait()
                 self.shared.append(share(self.image, self.far))
 
             def arrived(self):
@@ -193,9 +199,14 @@
             block = xrows(image, slot, c)
             return net.send(block, block, sib, s_like)
 
+        rest = (1, 2, 3)
+        own_c, own_s, part_c, part_s = [Ring(i, g, (0,)) for g in (zh, 1 - zh) for i in (c, s)]
+        own0, own1, ring0, ring1 = [Ring(i, g, rest) for g in (zh, 1 - zh) for i in (0, 1)]
         w_sib = net.send(w_ref.at[:, ds(s * HC, HC, 128)], wg.at[ds(chip * 192 + c * 96, 96, 32)], sib)
         x_sib = [net.send(x_ref.at[ds(h * 64, 64, 64)], xrows(c, seq, h), sib) for h in (s, c)]
-        parts = range(PARTS)
+        block = x_ref.at[ds(c * 64, PROWS, PROWS)]
+        own_c.send(0, block)
+        z_early = net.send(block, xrows(c, seq, c, 0), z_far, z_like)
         d_sib = net.send(d_ref.at[:, ds(s * HD, HD, 128)], dout.at[c], sib)
         t_sib = net.send(t_ref.at[:, ds(s * HC, HC, 128)], joined.at[c, pl.ds(0, TXT)], sib)
 
@@ -215,72 +226,77 @@
             for copy in (y_ring[k][1 - k % 2], y_ring[k][2]):
                 copy.wait_recv()
 
-        z = {}
-
-        def z_send(u):
-            block = xrows(u // PARTS, seq, c, u % PARTS)
-            z[u] = net.send(block, block, z_far, None if u in (4, 5) else z_like)
-
-        def step(ring, part):
-            z[ring.image * PARTS + part].wait_recv()
+        z = {(2, 0): z_early}
+
+        def z_send(image, part, key, source=None):
+            block = xrows(image, seq, c, part)
+            z[key, part] = net.send(source or block, block, z_far, z_like)
+
+        def step(ring, part, key):
+            z[key, part].wait_recv()
             ring.send(part)
 
         local[0].wait()
-        x_sib[0].wait_recv()
-        own0, own1, ring0, ring1 = Ring(0, zh), Ring(1, zh), Ring(0, 1 - zh), Ring(1, 1 - zh)
-        z_send(0)
-        for p in parts:
-            own0.send(p)
         local[1].wait()
         w_sib.wait_recv()
         block = wg.at[ds(chip * 192, 192, 64)]
         w_near = [net.send(block, block, peer, n_like) for peer in z_near]
-        for p in (1, 2, 3):
-            z_send(p)
+        x_sib[0].wait_recv()
+        own_s.send(0)
+        z_send(s, 0, 3)
+        for p in rest:
+            own0.send(p)
+        for p in rest:
+            z_send(0, p, 0)
         y_send(0)
-        own0.forward(0)
+        own_c.forward(0)
+        own_s.forward(0)
+        step(part_c, 0, 2)
         own0.forward(1)
-        step(ring0, 0)
         own0.forward(2)
         own0.forward(3)
         y_forward(0)
-        for p in parts:
+        for p in rest:
             own1.send(p)
+        own_c.near_wait()
+        own_s.near_wait()
         own0.share_near()
-        step(ring0, 1)
+        step(part_s, 0, 3)
+        own_c.far_wait()
+        own_s.far_wait()
         own0.share_far()
-        step(ring0, 2)
-        ring0.forward(0)
+        step(ring0, 1, 0)
+        part_c.forward(0)
         w_near[0].wait_recv()
         y_send(1)
         w_near[2].wait_recv()
         y_send(3)
-        step(ring0, 3)
+        step(ring0, 2, 0)
+        part_s.forward(0)
+        step(ring0, 3, 0)
         ring0.forward(1)
         w_near[1].wait_recv()
         y_send(2)
         for peer in z_near:
             pl.semaphore_signal(done_sem, inc=1, device_id=peer, device_id_type=MESH)
         pl.semaphore_wait(done_sem, 3)
-        z_send(4)
-        z_send(5)
+        for p in rest:
+            z_send(1, p, 1)
         far0 = share(0, ring0.mine)
-        own1.forward(0)
+        own1.forward(1)
         ring0.forward(2)
-        own1.forward(1)
         y_forward(1)
         ring0.forward(3)
         y_forward(3)
         own1.forward(2)
         y_forward(2)
+        part_c.near_wait()
+        part_s.near_wait()
         ring0.share_near()
         own1.forward(3)
-        net.sent(z[4])
-        z_send(6)
-        net.sent(z[5])
-        z_send(7)
-        step(ring1, 0)
-        step(ring1, 1)
+        step(ring1, 1, 1)
+        part_c.far_wait()
+        part_s.far_wait()
         ring0.share_far()
 
         def slots(image, first, count):
@@ -309,14 +325,13 @@
         own0.arrived()
         slots(0, zh * 4, 4)
         own1.share_near()
-        step(ring1, 2)
+        step(ring1, 2, 1)
         far0.wait_recv()
         ring0.arrived()
         slots(0, (1 - zh) * 4, 4)
-        step(ring1, 3)
+        step(ring1, 3, 1)
         own1.share_far()
         start(0)
-        ring1.forward(0)
         block(0, 0)
         ring1.forward(1)
         block(0, 1)

time: 112 us -> 111 us (level)
    pallas_call x1, Pallas kernels: 109 us -> 108 us  [per_device(): pl.pallas_call(make_kernel(), name='joint_block', out_shape=(jax.ShapeDty...]
where the time goes in v5:
time: 111 us
  Pallas kernels  108 us (97%)
  local copies, waits for them, and re-layouts  2.41 us (2%)
    pallas_call x1, Pallas kernels, per_device(): pl.pallas_call(make_kernel(), name='joint_block', out_shape=(jax.ShapeDty...  108 us
    unnamed x4, local copies, waits for them, and re-layouts  2.41 us

profile of v5, /device:TPU:1, one launch (start us, length us, event | category | flops | bytes accessed | tf_op | source)
XLA Modules:
  0.0 110.6 jit_solution(2746817769970208658)
XLA Ops:
  0.6 107.5 %joint_block.1 = (f32[96,768]{1,0:T(8,128)}, bf16[128,768]{1,0:T(8,128)(2,1)}) custom-call(bf16[128,3072]{1,0:T(8,128)(2,1)} %bitcast.6, bf16[128,768]{1,0:T(8,128)(2,1)} %bitcast.8, bf16[96,768]{1,0:T(8,128)(2,1)} %w_ref.1, f32[1,128]{1,0:T(1,128)} %bitcast.10, f32[1,128]{1,0:T(1,128)} %bitcast.11, bf16[1152,256]{1,0:T(8,128)(2,1)} %bitcast.7), custom_call_target="tpu_custom_call" | custom-call | tf_op jit(solution)/shard_map/joint_block/pallas_call | solution.py:444
  108.2 0.0 copy-start
  108.2 1.7 %copy.10 = f32[96,768]{1,0:T(8,128)} copy(f32[96,768]{1,0:T(8,128)} %get-tuple-element.8) | data formatting | bytes 589824
  109.9 0.0 copy-done
  109.9 0.7 copy.11
Async XLA Ops:
  108.2 1.7 %copy-start = (bf16[128,768]{1,0:T(8,128)(2,1)S(1)}, bf16[128,768]{1,0:T(8,128)(2,1)}, u32[]{:S(2)}) copy-start(bf16[128,768]{1,0:T(8,128)(2,1)} %get-tuple-element.5) | copy-start | bytes 589828
